TPU v7x, 256 devices: a whole 4x4x8 slice. The times are simulated.
256 devices in a mesh: seq: 32 (over x, y, core), tp: 8 (over z).
Axes of the slice: x: 4, y: 4, z: 8, core: 2. Of those that a mesh axis runs over, the one named last changes fastest.
Arguments:
- text_embed: bfloat16 [16384, 4096], P('seq', 'tp'), may hold values from -16 to 16
- latents: bfloat16 [32, 256, 64], P('seq'), may hold values from -6 to 6
- noise: bfloat16 [32, 256, 64], P('seq'), may hold values from -6 to 6
- timesteps: int32 [32], P('seq'), may hold values from 0 to 999
- image_block: int32 [32], replicated, may hold values from 0 to 63, as said below
- doc_ids: int32 [16384], replicated, may hold values from 0 to 3, never falling along the last dimension, each value on 1 to 14336 neighbouring positions
- norm_gain: float32 [4096], replicated, may hold values from 0.1 to 1.9
- w_patch: bfloat16 [64, 4096], P(None, 'tp'), may hold values from -0.75 to 0.75
- w_time: bfloat16 [256, 4096], P(None, 'tp'), may hold values from -0.375 to 0.375
- w_qkv: bfloat16 [4096, 3, 2048], P(None, None, 'tp'), may hold values from -3 to 3
- w_out: bfloat16 [2048, 4096], P('tp'), may hold values from -0.125 to 0.125
- w_dec: bfloat16 [4096, 64], P('tp'), may hold values from -0.09375 to 0.09375
Outputs:
- hidden_out: bfloat16 [16384, 4096], P('seq', 'tp')
- predicted: float32 [16384, 64], P('seq')
- patch_error: float32 [16384], P('seq')
Inputs may be any that keep to these rules, and one draw needn't show every extreme that they name: `image_block`: the blocks of different images are different.
All inputs are finite; a program needn't handle non-finite values.
Results may differ from a plain program's by a relative error of at most 0.024.
Values may be sent and summed in bfloat16 or wider, within the bound.
No kernel may reach another device: no remote copies, remote signals or barrier semaphores. Data moves between devices by JAX's collectives and lax.ppermute only.
A program may use at most 128 MiB of HBM per device.

v0:
```python
import math

import jax
import jax.numpy as jnp
from jax import lax
from jax.sharding import PartitionSpec as P

HD = 128
TSTEPS = 1000


epsilon = 1e-05
masked_score = -1e30


def noisy_patches(latents, noise, timesteps, freq_count):
    step_values = timesteps.astype(jnp.float32)
    signal_level = jnp.cos((step_values / TSTEPS + 0.008) / 1.008 * (math.pi / 2)) ** 2
    noised = (
        jnp.sqrt(signal_level)[:, None, None] * latents.astype(jnp.float32)
        + jnp.sqrt(1.0 - signal_level)[:, None, None] * noise.astype(jnp.float32)
    ).astype(jnp.bfloat16)
    frequencies = jnp.exp(
        -math.log(10000.0) * jnp.arange(freq_count, dtype=jnp.float32) / freq_count
    )
    angles = step_values[:, None] * frequencies[None, :]
    time_feats = jnp.concatenate([jnp.cos(angles), jnp.sin(angles)], axis=1).astype(jnp.bfloat16)
    return (noised, time_feats)


def embed_patches(noised, time_feats, w_patch, w_time):
    patch_part = jnp.einsum("ipc,cd->ipd", noised, w_patch, preferred_element_type=jnp.float32)
    time_part = jnp.dot(time_feats, w_time, preferred_element_type=jnp.float32)
    return (patch_part + time_part[:, None, :]).astype(jnp.bfloat16)


def per_device(
    text_embed,
    latents,
    noise,
    timesteps,
    image_block,
    doc_ids,
    norm_gain,
    w_patch,
    w_time,
    w_qkv,
    w_out,
    w_dec,
):
    seq_dev = text_embed.shape[0]
    local_width = text_embed.shape[1]
    patches = latents.shape[1]
    patch_values = latents.shape[2]
    width = norm_gain.shape[0]
    head_width = w_qkv.shape[2]
    heads_dev = head_width // HD
    blocks_dev = seq_dev // patches
    seq_count = lax.axis_size("seq")
    seq_index = lax.axis_index("seq")
    total_blocks = blocks_dev * seq_count
    image_count = image_block.shape[0]
    noised, time_feats = noisy_patches(latents, noise, timesteps, w_time.shape[0] // 2)
    local_blocks = seq_index * blocks_dev + jnp.arange(blocks_dev, dtype=jnp.int32)
    matches = image_block[None, :] == local_blocks[:, None]
    has_image = jnp.any(matches, axis=1)
    image_index = jnp.sum(
        jnp.where(matches, jnp.arange(image_count, dtype=jnp.int32)[None, :], 0), axis=1
    )
    every_noised, every_noise, every_feats = (
        lax.all_gather(noised, "seq", axis=0, tiled=True),
        lax.all_gather(noise, "seq", axis=0, tiled=True),
        lax.all_gather(time_feats, "seq", axis=0, tiled=True),
    )
    picked = embed_patches(every_noised[image_index], every_feats[image_index], w_patch, w_time)
    picked_noise = every_noise[image_index].astype(jnp.float32)
    text_blocks = text_embed.reshape(blocks_dev, patches, local_width)
    residual = jnp.where(has_image[:, None, None], picked, text_blocks).reshape(
        seq_dev, local_width
    )
    gathered = lax.all_gather(residual, "tp", axis=1, tiled=True).astype(jnp.float32)
    inverse = lax.rsqrt(jnp.mean(gathered * gathered, axis=1, keepdims=True) + epsilon)
    normed = (gathered * inverse * norm_gain[None, :]).astype(jnp.bfloat16)
    projected = jnp.dot(
        normed, w_qkv.reshape(width, 3 * head_width), preferred_element_type=jnp.float32
    )
    projected = projected.astype(jnp.bfloat16).reshape(seq_dev, 3, head_width)
    queries = projected[:, 0].reshape(seq_dev, heads_dev, HD)
    key_rows = projected[:, 1]
    value_rows = projected[:, 2]
    query_pos = seq_index * seq_dev + jnp.arange(seq_dev, dtype=jnp.int32)
    query_docs = lax.dynamic_slice_in_dim(doc_ids, seq_index * seq_dev, seq_dev, 0)
    query_blocks = query_pos // patches
    image_flags = jnp.any(
        image_block[None, :] == jnp.arange(total_blocks, dtype=jnp.int32)[:, None], axis=1
    )
    query_image = image_flags[query_blocks]
    score_scale = 1.0 / math.sqrt(HD)

    def block_update(running, key_block, value_block, first_key, block_rows):
        row_max, row_total, weighted = running
        key_pos = first_key + jnp.arange(block_rows, dtype=jnp.int32)
        key_docs = lax.dynamic_slice_in_dim(doc_ids, first_key, block_rows, 0)
        scores = (
            jnp.einsum(
                "qhd,khd->hqk",
                queries,
                key_block.reshape(block_rows, heads_dev, HD),
                preferred_element_type=jnp.float32,
            )
            * score_scale
        )
        allowed = (query_docs[:, None] == key_docs[None, :]) & (
            (key_pos[None, :] <= query_pos[:, None])
            | (key_pos[None, :] // patches == query_blocks[:, None]) & query_image[:, None]
        )
        scores = jnp.where(allowed[None], scores, masked_score)
        new_max = jnp.maximum(row_max, jnp.max(scores, axis=2))
        expo = jnp.where(allowed[None], jnp.exp(scores - new_max[:, :, None]), 0.0)
        rescale = jnp.exp(row_max - new_max)
        new_total = row_total * rescale + jnp.sum(expo, axis=2)
        contrib = jnp.einsum(
            "hqk,khd->hqd",
            expo.astype(jnp.bfloat16),
            value_block.reshape(block_rows, heads_dev, HD),
            preferred_element_type=jnp.float32,
        )
        return (new_max, new_total, weighted * rescale[:, :, None] + contrib)

    initial = (
        jnp.full((heads_dev, seq_dev), masked_score, jnp.float32),
        jnp.zeros((heads_dev, seq_dev), jnp.float32),
        jnp.zeros((heads_dev, seq_dev, HD), jnp.float32),
    )
    key_part = lax.all_gather(key_rows, "seq", axis=0, tiled=True)
    value_part = lax.all_gather(value_rows, "seq", axis=0, tiled=True)
    row_count = key_part.shape[0]
    block_rows = math.gcd(row_count, 512)
    block_count = row_count // block_rows
    key_blocks = key_part.reshape(block_count, block_rows, head_width)
    value_blocks = value_part.reshape(block_count, block_rows, head_width)
    offsets = jnp.arange(block_count, dtype=jnp.int32) * block_rows

    def fold_block(state_now, items):
        key_block, value_block, first_key = items
        updated = block_update(state_now, key_block, value_block, first_key, block_rows)
        return (updated, None)

    result, _ = lax.scan(fold_block, initial, (key_blocks, value_blocks, offsets))
    row_max, row_total, weighted = result
    attended = (weighted / row_total[:, :, None]).astype(jnp.bfloat16)
    attended = jnp.transpose(attended, (1, 0, 2)).reshape(seq_dev, head_width)
    head_term = jnp.dot(attended, w_out, preferred_element_type=jnp.float32)
    summed = lax.psum_scatter(
        head_term.astype(jnp.bfloat16), "tp", scatter_dimension=1, tiled=True
    ).astype(jnp.float32)
    hidden_out = (residual.astype(jnp.float32) + summed).astype(jnp.bfloat16)
    decode_part = jnp.dot(hidden_out, w_dec, preferred_element_type=jnp.float32)
    predicted = lax.psum(decode_part.astype(jnp.bfloat16), "tp").astype(jnp.float32)
    difference = predicted.reshape(blocks_dev, patches, patch_values) - picked_noise
    block_error = jnp.mean(difference * difference, axis=2)
    patch_error = jnp.where(has_image[:, None], block_error, 0.0).reshape(seq_dev)
    return (hidden_out, predicted, patch_error)


def solution(mesh):
    in_specs = (
        P("seq", "tp"),
        P("seq", None, None),
        P("seq", None, None),
        P("seq"),
        P(),
        P(),
        P(),
        P(None, "tp"),
        P(None, "tp"),
        P(None, None, "tp"),
        P("tp", None),
        P("tp", None),
    )
    out_specs = (P("seq", "tp"), P("seq", None), P("seq"))
    return jax.shard_map(
        per_device, mesh=mesh, in_specs=in_specs, out_specs=out_specs, check_vma=False
    )
```

profile of v0, /device:TPU:2, one launch (start us, length us, event | category | flops | bytes accessed | tf_op | source)
XLA Modules:
  0.0 853.4 jit_solution(14870340611683346652)
XLA Ops:
  9.7 24.2 %all-gather.2 = bf16[32,1,256]{2,1,0:T(2,128)(2,1)S(1)} all-gather(bf16[1,1,256]{2,1,0:T(2,128)(2,1)S(1)} %maximum_bitcast_fusion), channel_id=1, replica_groups=mesh['seq'=32,'tp'=8] {'seq'}, dimensions={0}, use_global_device_ids=true | all-gather | bytes 16896 | tf_op jit(solution)/shard_map/all_gather | solution.py:73
  37.2 24.4 %all-gather.9.cloned.1.call-done = bf16[32,256,64]{1,2,0:T(8,128)(2,1)} async-done(((bf16[1,256,64]{1,2,0:T(8,128)(2,1)}), bf16[32,256,64]{1,2,0:T(8,128)(2,1)}) %all-gather.9.cloned.1.call-update) | async-done | bytes 1048592 | tf_op jit(solution)/shard_map/all_gather | solution.py:71
  65.7 8.8 %copy.56 = bf16[4096,3,256]{0,2,1:T(8,128)(2,1)} copy(bf16[4096,3,256]{2,0,1:T(8,128)(2,1)} %param.23) | data formatting | bytes 12582912 | tf_op args[9]
  74.5 45.8 %all-gather.11.cloned.1.call-done = bf16[512,4096]{1,0:T(8,128)(2,1)} async-done(((bf16[512,512]{1,0:T(8,128)(2,1)}), bf16[512,4096]{1,0:T(8,128)(2,1)}) %all-gather.11.cloned.1.call-update) | async-done | bytes 4194320 | tf_op jit(solution)/shard_map/all_gather | solution.py:81
  123.7 7.1 fusion.30
  139.5 4.6 select_reduce_fusion
  144.1 35.6 %select_select_fusion = pred[512]{0:T(512)(128)(4,1)S(1)} fusion(pred[512]{0:T(512)(128)(4,1)S(1)} %get-tuple-element.427, pred[512]{0:T(512)(128)(4,1)S(1)} %get-tuple-element.428, pred[512]{0:T(512)(128)(4,1)S(1)} %get-tuple-element.429, pred[512]{0:T(512)(128)(4,1)S(1)} %get-tuple-element.430, pred[512]{0:T(512)(128)(4,1)S(1)} %get-tuple-element.431, ...), kind=kLoop, calls=%fused_computation.137 | loop fusion | flops 29184 | bytes 30265 | tf_op jit(solution)/shard_map/gather | solution.py:97
  180.0 16.4 %all-gather.15.cloned.1.call-done = bf16[16384,1,256]{0,2,1:T(8,128)(2,1)} async-done(((bf16[512,1,256]{0,2,1:T(8,128)(2,1)}), bf16[16384,1,256]{0,2,1:T(8,128)(2,1)}) %all-gather.15.cloned.1.call-update) | async-done | bytes 8388624 | tf_op jit(solution)/shard_map/all_gather | solution.py:135
  196.4 11.9 %copy.58 = bf16[16384,1,256]{2,0,1:T(8,128)(2,1)} copy(bf16[16384,1,256]{0,2,1:T(8,128)(2,1)} %all-gather.15.cloned.1.call-done) | data formatting | bytes 16777216 | tf_op jit(solution)/shard_map/all_gather | solution.py:135
  208.3 54.7 %all-gather.17.cloned.1.call-done = bf16[16384,1,256]{0,2,1:T(8,128)(2,1)} async-done(((bf16[512,1,256]{0,2,1:T(8,128)(2,1)}), bf16[16384,1,256]{0,2,1:T(8,128)(2,1)}) %all-gather.17.cloned.1.call-update) | async-done | bytes 8388624 | tf_op jit(solution)/shard_map/all_gather | solution.py:136
  263.0 11.9 %copy.59 = bf16[16384,1,256]{2,0,1:T(8,128)(2,1)} copy(bf16[16384,1,256]{0,2,1:T(8,128)(2,1)} %all-gather.17.cloned.1.call-done) | data formatting | bytes 16777216 | tf_op jit(solution)/shard_map/all_gather | solution.py:136
  274.8 436.7 %while.19 = (s32[]{:T(128)}, f32[2,512]{1,0:T(2,128)S(1)}, f32[2,512]{1,0:T(2,128)S(1)}, f32[2,512,128]{2,1,0:T(8,128)}, s32[512]{0:T(512)S(1)}, /*index=5*/s32[...) while((s32[]{:T(128)}, f32[2,512]{1,0:T(2,128)S(1)}, ...), condition=%wide.region_7.8_spmd.clone.clone.clone, body=%wide.region_4.7_spmd.clone.clone.clone.sunk | while | flops 277238784 | bytes 11363031 | solution.py:149
  298.6 3.4 convolution_add_fusion.3
  312.3 3.4 convolution_add_fusion.3
  325.9 3.4 convolution_add_fusion.3
  380.5 3.4 convolution_add_fusion.3
  448.8 3.4 convolution_add_fusion.3
  517.0 3.4 convolution_add_fusion.3
  585.3 3.4 convolution_add_fusion.3
  653.5 3.4 convolution_add_fusion.3
  694.4 3.4 convolution_add_fusion.3
  708.1 3.4 convolution_add_fusion.3
  718.0 53.6 %reduce-scatter.2.cloned.1.call-done = bf16[512,512]{1,0:T(8,128)(2,1)} async-done(((bf16[512,4096]{1,0:T(8,128)(2,1)}), bf16[512,512]{1,0:T(8,128)(2,1)}) %reduce-scatter.2.cloned.1.call-update) | async-done | bytes 524304 | tf_op jit(solution)/shard_map/reduce_scatter | solution.py:154
  773.8 70.6 %all-reduce.2.cloned.1.call-done = bf16[512,64]{0,1:T(8,128)(2,1)} async-done(((bf16[512,64]{0,1:T(8,128)(2,1)}), bf16[512,64]{0,1:T(8,128)(2,1)}) %all-reduce.2.cloned.1.call-update) | async-done | bytes 65552 | tf_op jit(solution)/shard_map/psum | solution.py:159
  (535 shorter events, 366.4 us)
Async XLA Ops:
  7.2 705.7 %copy-start = (bf16[256,4096]{1,0:T(8,128)(2,1)S(1)}, bf16[256,4096]{1,0:T(8,128)(2,1)}, u32[]{:S(2)}) copy-start(bf16[256,4096]{1,0:T(8,128)(2,1)} %param.24) | copy-start | bytes 6291460
  7.2 54.4 %all-gather.9.cloned.1.call-start = ((), (), s32[]{:S(2)}) async-start(), calls=%async_computation.1 | async-start | bytes 1081344 | tf_op jit(solution)/shard_map/all_gather | solution.py:71
  9.6 110.7 %all-gather.11.cloned.1.call-start = ((), (), s32[]{:S(2)}) async-start(), calls=%async_computation.2 | async-start | bytes 4718592 | tf_op jit(solution)/shard_map/all_gather | solution.py:81
  65.6 130.8 %all-gather.15.cloned.1.call-start = ((), (), s32[]{:S(2)}) async-start(), calls=%async_computation.6 | async-start | bytes 8650752 | tf_op jit(solution)/shard_map/all_gather | solution.py:135
  65.7 57.9 %copy-start.5 = (f32[4096]{0:T(1024)S(1)}, f32[4096]{0:T(1024)}, u32[]{:S(2)}) copy-start(f32[4096]{0:T(1024)} %param.20) | copy-start | bytes 49156
  120.3 3.4 copy-start.1
  130.9 3.7 copy-start.6
  133.2 129.8 %all-gather.17.cloned.1.call-start = ((), (), s32[]{:S(2)}) async-start(), calls=%async_computation.7 | async-start | bytes 8650752 | tf_op jit(solution)/shard_map/all_gather | solution.py:136
  133.8 582.4 %all-gather.13.cloned.1.call-start = ((), (), s32[]{:S(2)}) async-start(), calls=%async_computation.5 | async-start | bytes 1081344 | tf_op jit(solution)/shard_map/all_gather | solution.py:72
  134.4 637.2 %reduce-scatter.2.cloned.1.call-start = ((), (), s32[]{:S(2)}) async-start(), calls=%async_computation.3 | async-start | bytes 4718592 | tf_op jit(solution)/shard_map/reduce_scatter | solution.py:154
  716.0 55.6 %copy-start.3 = (bf16[2,256,512]{2,1,0:T(8,128)(2,1)S(1)}, bf16[2,256,512]{2,1,0:T(8,128)(2,1)}, u32[]{:S(2)}) copy-start(bf16[2,256,512]{2,1,0:T(8,128)(2,1)} %fusion.34) | copy-start | bytes 1572868
  716.0 56.8 %copy-start.4 = (bf16[512,64]{0,1:T(8,128)(2,1)S(1)}, bf16[512,64]{0,1:T(8,128)(2,1)}, u32[]{:S(2)}) copy-start(bf16[512,64]{0,1:T(8,128)(2,1)} %param.25) | copy-start | bytes 196612
  716.1 128.4 %all-reduce.2.cloned.1.call-start = ((), (), s32[]{:S(2)}) async-start(), calls=%async_computation.4 | async-start | bytes 131072 | tf_op jit(solution)/shard_map/psum | solution.py:159
  772.8 73.7 %copy-start.2 = (bf16[512,512]{1,0:T(8,128)(2,1)}, bf16[512,512]{1,0:T(8,128)(2,1)S(1)}, u32[]{:S(2)}) copy-start(bf16[512,512]{1,0:T(8,128)(2,1)S(1)} %add_convert_fusion) | copy-start | bytes 1572868
Sparse Core Ops, SparseCore 0:
  11.1 50.4 all-gather.8
  65.7 54.5 all-gather.10
  133.3 62.9 all-gather.14
  198.7 64.2 all-gather.16
  265.4 47.5 all-gather.12
  716.2 55.3 reduce-scatter.1
  774.5 69.9 all-reduce.1
where the time goes:
time: 861 us; the launch traced here: 853 us
  waiting for transfers between devices  267 us (31%)
  matrix products  187 us (22%)
  other arithmetic  158 us (18%)
  local copies, waits for them, and re-layouts  134 us (16%)
  loops' own time  67.7 us (8%)
  blocking collectives  24.2 us (3%)
  between operations  15.4 us (2%)
    dot_general x32, matrix products, block_update(): jnp.einsum('hqk,khd->hqd', expo.astype(jnp.bfloat16), value_block.reshape...  110 us
    psum x1, waiting for transfers between devices, per_device(): lax.psum(decode_part.astype(jnp.bfloat16), 'tp').astype(jnp.float32)  70.6 us
    reduce_sum x32, other arithmetic, block_update(): new_total = row_total * rescale + jnp.sum(expo, axis=2)  68.9 us
    another operation x1, loops' own time, per_device(): lax.scan(fold_block, initial, (key_blocks, value_blocks, offsets))  67.7 us
    dynamic_slice x128, local copies, waits for them, and re-layouts, per_device(): lax.scan(fold_block, initial, (key_blocks, value_blocks, offsets))  64.5 us
    dot_general x32, matrix products, block_update(): jnp.einsum('qhd,khd->hqk', queries, key_block.reshape(block_rows, heads_d...  63.1 us
    all_gather x1, waiting for transfers between devices, per_device(): value_part = lax.all_gather(value_rows, 'seq', axis=0, tiled=True)  54.7 us
    reduce_scatter x1, waiting for transfers between devices, per_device(): lax.psum_scatter(head_term.astype(jnp.bfloat16), 'tp', scatter_dimension=...  53.6 us
  transfers between devices with their start and end apart: 7, of which 6 were waited for; matrix products, arithmetic and copies ran while one was open for 53% of the time, Pallas kernels for 0%

commit v1 on v0

v1 whole, which is shorter than its diff:
```python
import functools
import math

import jax
import jax.numpy as jnp
from jax import lax
from jax.experimental import pallas as pl
from jax.experimental.pallas import tpu as pltpu
from jax.sharding import Mesh, PartitionSpec as P

HD = 128
TSTEPS = 1000
EPS = 1e-05
PATCH_ROWS = 256
BLOCKS = 64
IMAGES = 32
TEXTS = BLOCKS - IMAGES
STRIPES = 32
SROWS = 8
NZ = 8
WIDTH = 4096
LOCAL = WIDTH // NZ
S = BLOCKS * PATCH_ROWS
DOCS = 4
SEQ_AXES = ("x", "y", "c")
MASKED = -1e30
FLOOR = -1e29
SCALE2 = math.log2(math.e) / math.sqrt(HD)
QB = 4
KB = 8
VMEM = pl.BlockSpec(memory_space=pltpu.VMEM)
SMEM = pl.BlockSpec(memory_space=pltpu.SMEM)


def shifted(a, axis, shift):
    count = lax.axis_size(axis)
    return lax.ppermute(a, axis, [(i, (i + shift) % count) for i in range(count)])


def ring_eight(a):
    up = [a]
    down = [a]
    for _ in range(3):
        up.append(shifted(up[-1], "z", 1))
        down.append(shifted(down[-1], "z", -1))
    half = a.shape[0] // 2
    far_top = shifted(up[-1][:half], "z", 1)
    far_low = shifted(down[-1][half:], "z", -1)
    return up, down[1:], (far_top, far_low)


def nt_dot(a, b):
    return lax.dot_general(a, b, (((1,), (1,)), ((), ())), preferred_element_type=jnp.float32)


def qkv_kernel(
    sc_ref, slot_ref, u0, u1, u2, u3, d1, d2, d3, f0, f1, w_ref, gain_ref, wg_ref, noised_ref,
    mine_ref, other_ref, dec_ref, res_ref, acc_ref, dec_acc,
):
    z = sc_ref[3]
    c = sc_ref[2]
    rows_t = TEXTS * SROWS
    rows = BLOCKS * SROWS
    squares = jnp.zeros((rows, 1), jnp.float32)
    decoded = jnp.zeros((rows, 64), jnp.float32)
    shifts = (0, 1, 2, 3, -1, -2, -3, 4)
    refs = (u0, u1, u2, u3, d1, d2, d3, None)
    for k, (shift, ref) in enumerate(zip(shifts, refs)):
        src = lax.rem(z - shift + NZ, NZ)
        if ref is None:
            block = jnp.concatenate([f0[...], f1[...]], axis=0)
        else:
            block = ref[...]
        text = block[:rows_t]
        times = block[rows_t:].astype(jnp.float32)
        wp = wg_ref[src, 0:64, :]
        wd = wg_ref[src, 64:128, :]
        patch = jnp.dot(noised_ref[...], wp, preferred_element_type=jnp.float32)
        timed = jnp.broadcast_to(times[:, None, :], (IMAGES, SROWS, LOCAL)).reshape(
            IMAGES * SROWS, LOCAL
        )
        image = (patch + timed).astype(jnp.bfloat16)
        both = jnp.concatenate([text, image], axis=0)
        res_ref[k] = both
        wide = both.astype(jnp.float32)
        squares = squares + jnp.sum(wide * wide, axis=1, keepdims=True)
        decoded = decoded + nt_dot(both, wd)
    dec_acc[...] = decoded
    inverse = lax.rsqrt(squares * (1.0 / WIDTH) + EPS)
    total = None
    for k, shift in enumerate(shifts):
        src = lax.rem(z - shift + NZ, NZ)
        normed = (res_ref[k].astype(jnp.float32) * inverse * gain_ref[src]).astype(jnp.bfloat16)
        part = jnp.dot(normed, w_ref[src], preferred_element_type=jnp.float32)
        total = part if total is None else total + part
    for j in range(6):
        acc_ref[j] = total[:, j * HD : (j + 1) * HD]

    def arrange(pair, carry):
        first = pl.multiple_of(slot_ref[2 * pair] * SROWS, SROWS)
        second = pl.multiple_of(slot_ref[2 * pair + 1] * SROWS, SROWS)
        at = pl.ds(pl.multiple_of(pair * 2 * SROWS, 2 * SROWS), 2 * SROWS)
        for j in range(3):
            for ref, head in ((mine_ref, c), (other_ref, 1 - c)):
                index = 2 * j + head
                ref[j, at, :] = jnp.concatenate(
                    [acc_ref[index, pl.ds(first, SROWS), :], acc_ref[index, pl.ds(second, SROWS), :]],
                    axis=0,
                ).astype(jnp.bfloat16)
        dec_ref[pair] = jnp.concatenate(
            [dec_acc[pl.ds(first, SROWS), :], dec_acc[pl.ds(second, SROWS), :]], axis=1
        )
        return carry

    lax.fori_loop(0, BLOCKS // 2, arrange, 0)


def attend_kernel(
    sc_ref, start_ref, flag_ref, q0, q1, q2, q3, kv0, kv1, kv3, k2, v2, dec_ref, img_ref,
    out_ref, qs, ks, vs, m_ref, acc_ref,
):
    x, y, c = sc_ref[0], sc_ref[1], sc_ref[2]
    ones = jnp.ones((8, 512, HD), jnp.bfloat16)
    vs[:, :, HD:] = ones
    for i in range(2):
        cc = c if i == 0 else 1 - c
        for ref, shift in ((q0, 0), (q1, 1), (q2, 2), (q3, 3)):
            qs[lax.rem(y - shift + 4, 4) * 2 + cc] = ref[i]
        for ref, shift in ((kv0, 0), (kv1, 1), (kv3, 3)):
            at = lax.rem(x - shift + 4, 4) * 2 + cc
            ks[at] = ref[i, 0]
            vs[at, :, :HD] = ref[i, 1]
        at = lax.rem(x + 2, 4) * 2 + cc
        ks[at] = k2[i]
        vs[at, :, :HD] = v2[i]

    rows = QB * 64
    cols = KB * 64
    starts = [start_ref[d] for d in range(DOCS)]

    def doc_low(position):
        low = 0
        for start in starts:
            low = jnp.where(start <= position, jnp.maximum(start, low), low)
        return low

    def q_tile(i, carry):
        rho = lax.broadcasted_iota(jnp.int32, (rows, HD), 0)
        piece, blk, row = rho >> 5, (rho >> 3) & 3, rho & 7
        first = (QB * i + blk) * PATCH_ROWS
        q_pos = first + 64 * x + 8 * piece + row
        low = jnp.zeros((rows, HD), jnp.int32)
        high_doc = jnp.full((rows, HD), S - 1, jnp.int32)
        for start in starts:
            low = jnp.where(start <= q_pos, jnp.maximum(low, start), low)
            high_doc = jnp.where(start > q_pos, jnp.minimum(high_doc, start - 1), high_doc)
        flag = jnp.zeros((rows, HD), jnp.int32)
        for n in range(QB):
            flag = jnp.where(blk == n, flag_ref[QB * i + n], flag)
        high = jnp.where(flag == 1, jnp.minimum(high_doc, first + PATCH_ROWS - 1), q_pos)
        low_col, high_col = low[:, :1], high[:, :1]
        m_ref[...] = jnp.full((rows, HD), FLOOR, jnp.float32)
        acc_ref[...] = jnp.zeros((rows, 2 * HD), jnp.float32)
        q_at = pl.ds(pl.multiple_of(i * QB * SROWS, QB * SROWS), QB * SROWS)
        low_first = doc_low(i * (QB * PATCH_ROWS))
        low_last = doc_low(i * (QB * PATCH_ROWS) + QB * PATCH_ROWS - 1)
        last = (i * QB) // KB

        def k_tile(j, inner):
            k_at = pl.ds(pl.multiple_of(j * KB * SROWS, KB * SROWS), KB * SROWS)
            full = jnp.logical_and(j < last, low_last <= j * (KB * PATCH_ROWS))

            def fold(masked):
                q = qs[:, q_at, :].reshape(rows, HD)
                k = ks[:, k_at, :].reshape(cols, HD)
                s = nt_dot(q, k)
                if masked:
                    kappa = lax.broadcasted_iota(jnp.int32, (1, cols), 1)
                    k_pos = (
                        (KB * j + ((kappa >> 3) & 7)) * PATCH_ROWS
                        + 64 * (kappa >> 7) + 16 * y + 8 * ((kappa >> 6) & 1) + (kappa & 7)
                    )
                    seen = jnp.logical_and(k_pos >= low_col, k_pos <= high_col)
                    s = jnp.where(seen, s, MASKED)
                m_old = m_ref[...]
                m_new = jnp.maximum(m_old, jnp.max(s, axis=1, keepdims=True))
                m_ref[...] = m_new
                p = jnp.exp2((s - m_new[:, :1]) * SCALE2).astype(jnp.bfloat16)
                alpha = jnp.exp2((m_old - m_new) * SCALE2)
                pv = jnp.dot(
                    p, vs[:, k_at, :].reshape(cols, 2 * HD), preferred_element_type=jnp.float32
                )
                acc_ref[...] = acc_ref[...] * jnp.concatenate([alpha, alpha], axis=1) + pv

            @pl.when(full)
            def _():
                fold(False)

            @pl.when(jnp.logical_not(full))
            def _():
                fold(True)

            return inner

        lax.fori_loop(low_first // (KB * PATCH_ROWS), last + 1, k_tile, 0)
        total = acc_ref[:, HD:]
        some = total > 0.0
        safe = jnp.where(some, total, 1.0)
        o = (acc_ref[:, :HD] / safe).astype(jnp.bfloat16).reshape(8, QB * SROWS, HD)
        level = jnp.where(some, m_ref[...] * SCALE2 + jnp.log2(safe), MASKED)
        level = level.reshape(8, QB * SROWS, HD)
        which = lax.broadcasted_iota(jnp.int32, (8, HD), 0)
        for d in range(QB // 2):
            dest = (QB // 2) * i + d
            out_ref[dest, 0:8] = o[:, 16 * d : 16 * d + 16, :]
            line = jnp.transpose(level[:, 16 * d : 16 * d + 16, :].reshape(HD, HD))[:8]
            high_part = line.astype(jnp.bfloat16).astype(jnp.float32)
            rest = line - high_part
            mid_part = rest.astype(jnp.bfloat16).astype(jnp.float32)
            low_part = rest - mid_part
            head = jnp.where(which == 0, high_part, jnp.where(which == 1, mid_part, low_part))
            out_ref[dest, 8] = jnp.concatenate([head, dec_ref[dest]], axis=0).astype(jnp.bfloat16)
            out_ref[dest, 9] = img_ref[dest]
        return carry

    lax.fori_loop(0, BLOCKS // QB, q_tile, 0)


def combine_kernel(in_ref, w2_ref, att_ref, dec_ref, full_ref):
    for x in range(4):
        for c in range(2):
            heads = [in_ref[x * 8 + y * 2 + c, 8].astype(jnp.float32) for y in range(4)]
            levels = [h[0:1] + h[1:2] + h[2:3] for h in heads]
            top = functools.reduce(jnp.maximum, levels)
            weights = [jnp.exp2(level - top) for level in levels]
            total = functools.reduce(jnp.add, weights)
            part = None
            for y in range(4):
                share = jnp.transpose(jnp.broadcast_to(weights[y] / total, (HD, HD)))
                o = in_ref[x * 8 + y * 2 + c, 0:8].reshape(HD, HD).astype(jnp.float32)
                part = o * share if part is None else part + o * share
            for p in range(8):
                for b in range(2):
                    full_ref[
                        b * PATCH_ROWS + 64 * x + 8 * p : b * PATCH_ROWS + 64 * x + 8 * p + 8,
                        c * HD : (c + 1) * HD,
                    ] = part[(2 * p + b) * 8 : (2 * p + b) * 8 + 8]
            for y in range(4):
                stripe = x * 8 + y * 2 + c
                for b in range(2):
                    at = b * PATCH_ROWS + stripe * SROWS
                    dec_ref[at : at + SROWS, :] = heads[y][8:16, b * 64 : (b + 1) * 64]
    att_ref[0:512, :] = full_ref[...].astype(jnp.bfloat16)
    att_ref[512:576, :] = w2_ref[...]


def kernel_params(mib):
    return pltpu.CompilerParams(vmem_limit_bytes=mib * 1024 * 1024)


def per_device(
    text_embed, latents, noise, timesteps, image_block, doc_ids, norm_gain,
    w_patch, w_time, w_qkv, w_out, w_dec,
):
    ix, iy, ic, iz = (lax.axis_index(a) for a in ("x", "y", "c", "z"))
    seq = ix * 8 + iy * 2 + ic
    f32, bf16 = jnp.float32, jnp.bfloat16
    scalars = jnp.stack([ix, iy, ic, iz]).astype(jnp.int32)

    out_slice = lax.dynamic_slice_in_dim(w_out, seq * 8, 8, 0).reshape(64, LOCAL)
    packed = jnp.concatenate([w_patch, w_dec.T, out_slice], axis=0)
    wg = lax.all_gather(packed, "z", axis=0, tiled=False)

    step = timesteps.astype(f32)
    signal = jnp.cos((step / TSTEPS + 0.008) / 1.008 * (math.pi / 2)) ** 2
    noised = (
        jnp.sqrt(signal)[:, None, None] * latents.astype(f32)
        + jnp.sqrt(1.0 - signal)[:, None, None] * noise.astype(f32)
    ).astype(bf16)
    freq_count = w_time.shape[0] // 2
    freqs = jnp.exp(-math.log(10000.0) * jnp.arange(freq_count, dtype=f32) / freq_count)
    angles = step[:, None] * freqs[None, :]
    feats = jnp.concatenate([jnp.cos(angles), jnp.sin(angles)], axis=1).astype(bf16)

    text_part = (
        text_embed.reshape(2, STRIPES, SROWS, LOCAL)
        .transpose(1, 0, 2, 3)
        .reshape(STRIPES, 2 * SROWS, LOCAL)
    )
    feat_row = jnp.pad(feats, ((0, 0), (0, 256)))
    image_part = jnp.stack(
        [
            noised.reshape(STRIPES, 512),
            noise.reshape(STRIPES, 512),
            jnp.broadcast_to(feat_row, (STRIPES, 512)),
            jnp.zeros((STRIPES, 512), bf16),
        ],
        axis=1,
    )
    sent = jnp.concatenate([text_part, image_part], axis=1)
    got = lax.all_to_all(sent, SEQ_AXES, 0, 0, tiled=False)

    block_ids = jnp.arange(BLOCKS, dtype=jnp.int32)
    matches = image_block[None, :] == block_ids[:, None]
    flags = jnp.any(matches, axis=1)
    image_of = jnp.sum(jnp.where(matches, jnp.arange(IMAGES, dtype=jnp.int32)[None, :], 0), axis=1)
    rank = jnp.sum(
        jnp.where((block_ids[None, :] < block_ids[:, None]) & ~flags[None, :], 1, 0), axis=1
    )
    slots = jnp.where(flags, TEXTS + image_of, rank).astype(jnp.int32)
    text_ids = jnp.arange(TEXTS, dtype=jnp.int32)
    text_block = jnp.sum(
        jnp.where((rank[None, :] == text_ids[:, None]) & ~flags[None, :], block_ids[None, :], 0),
        axis=1,
    )
    doc_start = jnp.sum(
        (doc_ids[None, :] < jnp.arange(DOCS, dtype=jnp.int32)[:, None]).astype(jnp.int32), axis=1
    )
    flag_ints = flags.astype(jnp.int32)

    text_rows = got[:, :16].reshape(BLOCKS, SROWS, LOCAL)[text_block].reshape(-1, LOCAL)
    every_feats = got[:, 18, :256]
    time_part = jnp.dot(every_feats, w_time, preferred_element_type=f32)
    payload = jnp.concatenate([text_rows, time_part.astype(bf16)], axis=0)
    up, down, far = ring_eight(payload)

    noised_rows = got[:, 16].reshape(IMAGES * SROWS, 64)
    noise_rows = got[:, 17].reshape(IMAGES * SROWS, 64)
    pair_rows = jnp.concatenate([noised_rows, noise_rows], axis=1).reshape(IMAGES, SROWS, 128)
    image_back = pair_rows[image_of].reshape(STRIPES, 2 * SROWS, 128)

    w_cols, _ = lax.optimization_barrier((w_qkv, got))
    w_cols = w_cols.reshape(NZ, LOCAL, 6 * HD)
    gains = norm_gain.reshape(NZ, 1, LOCAL)

    mine, other, dec_rows = pl.pallas_call(
        qkv_kernel,
        out_shape=(
            jax.ShapeDtypeStruct((3, BLOCKS * SROWS, HD), bf16),
            jax.ShapeDtypeStruct((3, BLOCKS * SROWS, HD), bf16),
            jax.ShapeDtypeStruct((STRIPES, SROWS, 128), f32),
        ),
        in_specs=[SMEM, SMEM] + [VMEM] * 13,
        out_specs=(VMEM, VMEM, VMEM),
        scratch_shapes=[
            pltpu.VMEM((NZ, BLOCKS * SROWS, LOCAL), bf16),
            pltpu.VMEM((6, BLOCKS * SROWS, HD), f32),
            pltpu.VMEM((BLOCKS * SROWS, 64), f32),
        ],
        compiler_params=kernel_params(48),
        name="qkv",
    )(scalars, slots, *up, *down, *far, w_cols, gains, wg, noised_rows)

    theirs = lax.ppermute(other, "c", [(0, 1), (1, 0)])
    pieces = jnp.stack([mine, theirs])
    q = pieces[:, 0]
    kv = pieces[:, 1:]
    k = pieces[:, 1]
    v = pieces[:, 2]
    q1, q3 = shifted(q, "y", 1), shifted(q, "y", -1)
    kv1, kv3 = shifted(kv, "x", 1), shifted(kv, "x", -1)
    q2 = shifted(q, "y", 2)
    k2, v2 = shifted(k, "x", 2), shifted(v, "x", 2)

    partial = pl.pallas_call(
        attend_kernel,
        out_shape=jax.ShapeDtypeStruct((STRIPES, 10, 16, HD), bf16),
        in_specs=[SMEM, SMEM, SMEM] + [VMEM] * 11,
        out_specs=VMEM,
        scratch_shapes=[
            pltpu.VMEM((8, 512, HD), bf16),
            pltpu.VMEM((8, 512, HD), bf16),
            pltpu.VMEM((8, 512, 2 * HD), bf16),
            pltpu.VMEM((QB * 64, HD), f32),
            pltpu.VMEM((QB * 64, 2 * HD), f32),
        ],
        compiler_params=kernel_params(48),
        name="attend",
    )(scalars, doc_start, flag_ints, q, q1, q2, q3, kv, kv1, kv3, k2, v2, dec_rows, image_back)
    parts = lax.all_to_all(partial, SEQ_AXES, 0, 0, tiled=False)

    own = lax.dynamic_index_in_dim(wg[:, 128:].reshape(NZ, 8, NZ, LOCAL), iz, 2, keepdims=False)
    out_cols = lax.all_gather(own, SEQ_AXES, axis=0, tiled=False)
    out_cols = out_cols.transpose(1, 0, 2, 3).reshape(NZ, 2 * HD, LOCAL)
    w_dec_t = wg[:, 64:128].transpose(1, 0, 2).reshape(64, WIDTH)
    w2_t = nt_dot(w_dec_t, w_out).astype(bf16)

    att, dec_own = pl.pallas_call(
        combine_kernel,
        out_shape=(
            jax.ShapeDtypeStruct((576, 2 * HD), bf16),
            jax.ShapeDtypeStruct((512, 64), f32),
        ),
        in_specs=[VMEM, VMEM],
        out_specs=(VMEM, VMEM),
        scratch_shapes=[pltpu.VMEM((512, 2 * HD), f32)],
        compiler_params=kernel_params(32),
        name="combine",
    )(parts, w2_t)

    up, down, far = ring_eight(att)
    own_images = (
        parts[:, 9].reshape(STRIPES, 2, SROWS, 128).transpose(1, 0, 2, 3).reshape(512, 128)
    )
    own_noised, own_noise = own_images[:, :64], own_images[:, 64:].astype(f32)
    own_blocks = 2 * seq + jnp.arange(2, dtype=jnp.int32)
    own_times = time_part[image_of[own_blocks]]
    own_flags = flags[own_blocks]
    embedded = (
        jnp.dot(own_noised, w_patch, preferred_element_type=f32).reshape(2, PATCH_ROWS, LOCAL)
        + own_times[:, None, :]
    ).astype(bf16)
    residual = jnp.where(
        own_flags[:, None, None], embedded, text_embed.reshape(2, PATCH_ROWS, LOCAL)
    ).reshape(512, LOCAL)

    blocks = list(zip(up, (0, 1, 2, 3))) + list(zip(down, (-1, -2, -3)))
    blocks.append((jnp.concatenate(far, axis=0), 4))
    hidden = residual.astype(f32)
    predicted = dec_own
    for block, shift in blocks:
        src = lax.rem(iz - shift + NZ, NZ)
        w_part = lax.dynamic_index_in_dim(out_cols, src, 0, keepdims=False)
        hidden = hidden + jnp.dot(block[:512], w_part, preferred_element_type=f32)
        predicted = predicted + nt_dot(block[:512], block[512:])
    hidden_out = hidden.astype(bf16)
    difference = predicted - own_noise
    error = jnp.mean(difference * difference, axis=1).reshape(2, PATCH_ROWS)
    patch_error = jnp.where(own_flags[:, None], error, 0.0).reshape(512)
    return hidden_out, predicted, patch_error


def solution(mesh):
    fine = Mesh(mesh.devices.reshape(4, 4, 2, NZ), ("x", "y", "c", "z"))
    seq, tp = SEQ_AXES, "z"
    in_specs = (
        P(seq, tp),
        P(seq, None, None),
        P(seq, None, None),
        P(seq),
        P(),
        P(),
        P(),
        P(None, tp),
        P(None, tp),
        P(None, None, tp),
        P(tp, None),
        P(tp, None),
    )
    out_specs = (P(seq, tp), P(seq, None), P(seq))
    return jax.shard_map(
        per_device, mesh=fine, in_specs=in_specs, out_specs=out_specs, check_vma=False
    )
```

time: 861 us -> 297 us (0.34)
  waiting for transfers between devices: 267 us -> 78.7 us
  matrix products: 187 us -> 8.3 us
  other arithmetic: 158 us -> 8.64 us
  local copies, waits for them, and re-layouts: 134 us -> 61.3 us
  loops' own time: 67.7 us -> 0 us
  Pallas kernels: 0 us -> 66.5 us
  starting transfers between devices: 0.46 us -> 52.6 us
  blocking collectives: 24.2 us -> 0 us
    dot_general x69 -> x19, matrix products: 187 us -> 8.3 us  [the longest x8 3.15 us: per_device(): hidden = hidden + jnp.dot(block[:512], w_part, preferred_element_type=f32)]
    all_gather x5 -> x2, waiting for transfers between devices: 141 us -> 0.02 us  [the longest x1 0.02 us: per_device(): wg = lax.all_gather(packed, 'z', axis=0, tiled=False)]
    dynamic_slice x161 -> x2, local copies, waits for them, and re-layouts: 90.1 us -> 0.15 us  [the longest x1 0.14 us: per_device(): lax.dynamic_index_in_dim(wg[:, 128:].reshape(NZ, 8, NZ, LOCAL), iz, 2, ke...]
    reduce_sum x35 -> x4, other arithmetic: 74.5 us -> 1.41 us  [the longest x1 1.09 us: per_device(): jnp.sum((doc_ids[None, :] < jnp.arange(DOCS, dtype=jnp.int32)[:, None]).a...]
    psum x1 -> x0, waiting for transfers between devices: 70.6 us -> none  [per_device(): lax.psum(decode_part.astype(jnp.bfloat16), 'tp').astype(jnp.float32)]
    another operation x1 -> x0, loops' own time: 67.7 us -> none  [per_device(): lax.scan(fold_block, initial, (key_blocks, value_blocks, offsets))]
    pallas_call x0 -> x3, Pallas kernels: none -> 66.5 us  [the longest x1 53.9 us: per_device(): pl.pallas_call(attend_kernel, out_shape=jax.ShapeDtypeStruct((STRIPES, 10...]
    ppermute x0 -> x24, waiting for transfers between devices: none -> 53.6 us  [the longest x23 51.7 us: shifted(): lax.ppermute(a, axis, [(i, (i + shift) % count) for i in range(count)])]
  transfers between devices with their start and end apart: 7 -> 28, of which waited for: 6 -> 12; matrix products, arithmetic and copies ran while one was open for 53% -> 21% of each run, Pallas kernels for 0% -> 19%
where the time goes in v1:
time: 297 us; the launch traced here: 292 us
  waiting for transfers between devices  78.7 us (26%)
  Pallas kernels  66.5 us (22%)
  local copies, waits for them, and re-layouts  61.3 us (21%)
  starting transfers between devices  52.6 us (18%)
  between operations  15.5 us (5%)
  other arithmetic  8.64 us (3%)
  matrix products  8.3 us (3%)
    pallas_call x1, Pallas kernels, per_device(): pl.pallas_call(attend_kernel, out_shape=jax.ShapeDtypeStruct((STRIPES, 10...  53.9 us
    ppermute x23, waiting for transfers between devices, shifted(): lax.ppermute(a, axis, [(i, (i + shift) % count) for i in range(count)])  51.7 us
    ppermute x23, starting transfers between devices, shifted(): lax.ppermute(a, axis, [(i, (i + shift) % count) for i in range(count)])  38.9 us
    reshape x2, local copies, waits for them, and re-layouts, per_device(): w_cols = w_cols.reshape(NZ, LOCAL, 6 * HD)  28 us
    unnamed x76, local copies, waits for them, and re-layouts  13.5 us
    all_to_all x1, waiting for transfers between devices, per_device(): parts = lax.all_to_all(partial, SEQ_AXES, 0, 0, tiled=False)  13.4 us
    pallas_call x1, Pallas kernels, per_device(): pl.pallas_call(qkv_kernel, out_shape=(jax.ShapeDtypeStruct((3, BLOCKS * S...  12 us
    all_to_all x1, waiting for transfers between devices, per_device(): got = lax.all_to_all(sent, SEQ_AXES, 0, 0, tiled=False)  11.6 us
  transfers between devices with their start and end apart: 28, of which 12 were waited for; matrix products, arithmetic and copies ran while one was open for 21% of the time, Pallas kernels for 19%

profile of v1, /device:TPU:2, one launch (start us, length us, event | category | flops | bytes accessed | tf_op | source)
XLA Modules:
  0.0 291.6 jit_solution(3959330549470313307)
XLA Ops:
  17.0 7.6 %all-to-all-start = ((bf16[32,20,512]{2,1,0:T(8,128)(2,1)}), bf16[32,20,512]{2,1,0:T(8,128)(2,1)S(1)}, u32[]{:S(2)}, u32[]{:S(2)}) async-start(bf16[32,20,512]{2,1,0:T(8,128)(2,1)} %concatenate.39), calls=%async_computation | async-start | bytes 1572864 | tf_op jit(solution)/shard_map/all_to_all | solution.py:301
  25.1 11.6 %all-to-all-done = bf16[32,20,512]{2,1,0:T(8,128)(2,1)S(1)} async-done(((bf16[32,20,512]{2,1,0:T(8,128)(2,1)}), bf16[32,20,512]{2,1,0:T(8,128)(2,1)S(1)}, u32[]{:S(2)}, u32[]{:S(2)}) %all-to-all-start) | async-done | bytes 655392 | tf_op jit(solution)/shard_map/all_to_all | solution.py:301
  42.8 4.0 %collective-permute-start.3 = (bf16[288,512]{1,0:T(8,128)(2,1)S(1)}, bf16[288,512]{1,0:T(8,128)(2,1)S(1)}, u32[]{:S(2)}, u32[]{:S(2)}) collective-permute-start(bf16[288,512]{1,0:T(8,128)(2,1)S(1)} %pad_maximum_fusion.u0), channel_id=1, source_target_pairs={{0,7},{1,0},{2,1},{3,2},{4,3},{5,4},{6,5},{7,6},{8,15},{9,8},{10,9... | collective-permute-start | bytes 884744 | tf_op jit(solution)/shard_map/ppermute | solution.py:37
  46.8 9.7 %collective-permute-done.u1 = bf16[288,512]{1,0:T(8,128)(2,1)S(1)} collective-permute-done((bf16[288,512]{1,0:T(8,128)(2,1)S(1)}, bf16[288,512]{1,0:T(8,128)(2,1)S(1)}, u32[]{:S(2)}, u32[]{:S(2)}) %collective-permute-start) | collective-permute-done | bytes 294944 | tf_op jit(solution)/shard_map/ppermute | solution.py:37
  56.5 3.2 %collective-permute-start.4 = (bf16[288,512]{1,0:T(8,128)(2,1)S(1)}, bf16[288,512]{1,0:T(8,128)(2,1)}, u32[]{:S(2)}, u32[]{:S(2)}) collective-permute-start(bf16[288,512]{1,0:T(8,128)(2,1)S(1)} %collective-permute-done.3.d1), channel_id=1, source_target_pairs={{0,7},{1,0},{2,1},{3,2},{4,3},{5,4},{6,5},{7,6},{8,15},{9,8},{10,9... | collective-permute-start | bytes 884744 | tf_op jit(solution)/shard_map/ppermute | solution.py:37
  60.4 6.4 %collective-permute-done.1.u2 = bf16[288,512]{1,0:T(8,128)(2,1)} collective-permute-done((bf16[288,512]{1,0:T(8,128)(2,1)S(1)}, bf16[288,512]{1,0:T(8,128)(2,1)}, u32[]{:S(2)}, u32[]{:S(2)}) %collective-permute-start.1) | collective-permute-done | bytes 294944 | tf_op jit(solution)/shard_map/ppermute | solution.py:37
  66.8 3.2 %collective-permute-start.5 = (bf16[288,512]{1,0:T(8,128)(2,1)}, bf16[288,512]{1,0:T(8,128)(2,1)S(1)}, u32[]{:S(2)}, u32[]{:S(2)}) collective-permute-start(bf16[288,512]{1,0:T(8,128)(2,1)} %collective-permute-done.4.d2), channel_id=1, source_target_pairs={{0,7},{1,0},{2,1},{3,2},{4,3},{5,4},{6,5},{7,6},{8,15},{9,8},{10,9... | collective-permute-start | bytes 884744 | tf_op jit(solution)/shard_map/ppermute | solution.py:37
  70.2 6.3 %collective-permute-done.2.u3 = bf16[288,512]{1,0:T(8,128)(2,1)S(1)} collective-permute-done((bf16[288,512]{1,0:T(8,128)(2,1)}, bf16[288,512]{1,0:T(8,128)(2,1)S(1)}, u32[]{:S(2)}, u32[]{:S(2)}) %collective-permute-start.2) | collective-permute-done | bytes 294944 | tf_op jit(solution)/shard_map/ppermute | solution.py:37
  77.8 3.2 %collective-permute-start.7 = (bf16[144,512]{1,0:T(8,128)(2,1)}, bf16[144,512]{1,0:T(8,128)(2,1)}, u32[]{:S(2)}, u32[]{:S(2)}) collective-permute-start(bf16[144,512]{1,0:T(8,128)(2,1)} %slice.153), channel_id=1, source_target_pairs={{0,7},{1,0},{2,1},{3,2},{4,3},{5,4},{6,5},{7,6},{8,15},{9,8},{10,9... | collective-permute-start | bytes 442376 | tf_op jit(solution)/shard_map/ppermute | solution.py:37
  82.7 10.5 %copy.130 = bf16[4096,3,256]{2,1,0:T(4,128)(2,1)} copy(bf16[4096,3,256]{2,0,1:T(8,128)(2,1)} %param.21) | data formatting | bytes 12582912 | tf_op jit(solution)/shard_map/reshape | solution.py:333
  93.2 17.5 %reshape.221.w_ref = bf16[8,512,768]{2,1,0:T(8,128)(2,1)} reshape(bf16[4096,3,256]{2,1,0:T(4,128)(2,1)} %copy.130) | data formatting | bytes 12582912 | tf_op jit(solution)/shard_map/reshape | solution.py:333
  114.0 12.0 %qkv.1 = (bf16[3,512,128]{2,1,0:T(8,128)(2,1)S(1)}, bf16[3,512,128]{2,1,0:T(8,128)(2,1)}, f32[32,8,128]{2,1,0:T(8,128)S(1)}) custom-call(s32[4]{0:T(128)S(1)} %pad_add_fusion.sc_ref, s32[64]{0:T(128)S(1)} %add_select_fusion.slot_ref, bf16[288,512]{1,0:T(8,128)(2,1)S(1)} %pad_maximum_fusion.u0, bf16[288,512]{1,0:T(8,128)(2,1)S(1)} %copy-done.7, ...), custom_call_target="tpu_custom_call" | custom-call | tf_op jit(solution)/shard_map/qkv/pallas_call | solution.py:336
  139.3 4.4 %collective-permute-done.12 = bf16[2,2,512,128]{3,2,0,1:T(8,128)(2,1)} collective-permute-done((bf16[2,2,512,128]{3,2,0,1:T(8,128)(2,1)}, bf16[2,2,512,128]{3,2,0,1:T(8,128)(2,1)}, u32[]{:S(2)}, u32[]{:S(2)}) %collective-permute-start.12) | collective-permute-done | bytes 524320 | tf_op jit(solution)/shard_map/ppermute | solution.py:37
  154.9 3.8 %collective-permute-done.15.v2 = bf16[2,512,128]{2,1,0:T(8,128)(2,1)} collective-permute-done((bf16[2,512,128]{2,1,0:T(8,128)(2,1)}, bf16[2,512,128]{2,1,0:T(8,128)(2,1)}, u32[]{:S(2)}, u32[]{:S(2)}) %collective-permute-start.15) | collective-permute-done | bytes 262176 | tf_op jit(solution)/shard_map/ppermute | solution.py:37
  158.7 53.9 %attend.1 = bf16[32,10,16,128]{3,2,1,0:T(8,128)(2,1)S(1)} custom-call(s32[4]{0:T(128)S(1)} %pad_add_fusion.sc_ref, s32[4]{0:T(128)S(1)} %convert_reduce_fusion.start_ref, s32[64]{0:T(128)S(1)} %get-tuple-element.38.flag_ref, bf16[2,512,128]{2,1,0:T(8,128)(2,1)S(1)} %get-tuple-element.35.q0, bf16[2,512,128]{2,1,0:T(8,128)(2,1)S(1)} %collective-permute-done.9.q1, ...), custom_call_target="tpu_custom_call" | custom-call | tf_op jit(solution)/shard_map/attend/pallas_call | solution.py:365
  213.6 6.1 %all-to-all-start.1 = ((bf16[32,10,16,128]{3,2,1,0:T(8,128)(2,1)}), bf16[32,10,16,128]{3,2,1,0:T(8,128)(2,1)S(1)}, u32[]{:S(2)}, u32[]{:S(2)}) async-start(bf16[32,10,16,128]{3,2,1,0:T(8,128)(2,1)} %copy-done.1), calls=%async_computation.1 | async-start | bytes 2621440 | tf_op jit(solution)/shard_map/all_to_all | solution.py:380
  223.6 13.4 %all-to-all-done.1.in_ref = bf16[32,10,16,128]{3,2,1,0:T(8,128)(2,1)S(1)} async-done(((bf16[32,10,16,128]{3,2,1,0:T(8,128)(2,1)}), bf16[32,10,16,128]{3,2,1,0:T(8,128)(2,1)S(1)}, u32[]{:S(2)}, u32[]{:S(2)}) %all-to-all-start.1) | async-done | bytes 1310752 | tf_op jit(solution)/shard_map/all_to_all | solution.py:380
  237.8 3.2 %collective-permute-start.19 = (bf16[576,256]{1,0:T(8,128)(2,1)S(1)}, bf16[576,256]{1,0:T(8,128)(2,1)S(1)}, u32[]{:S(2)}, u32[]{:S(2)}) collective-permute-start(bf16[576,256]{1,0:T(8,128)(2,1)S(1)} %get-tuple-element.13), channel_id=1, source_target_pairs={{0,7},{1,0},{2,1},{3,2},{4,3},{5,4},{6,5},{7,6},{8,15},{9,8},{10,9... | collective-permute-start | bytes 884744 | tf_op jit(solution)/shard_map/ppermute | solution.py:37
  241.4 7.1 %collective-permute-done.16 = bf16[576,256]{1,0:T(8,128)(2,1)S(1)} collective-permute-done((bf16[576,256]{1,0:T(8,128)(2,1)S(1)}, bf16[576,256]{1,0:T(8,128)(2,1)S(1)}, u32[]{:S(2)}, u32[]{:S(2)}) %collective-permute-start.16) | collective-permute-done | bytes 294944 | tf_op jit(solution)/shard_map/ppermute | solution.py:37
  248.6 3.2 %collective-permute-start.20 = (bf16[576,256]{1,0:T(8,128)(2,1)S(1)}, bf16[576,256]{1,0:T(8,128)(2,1)S(1)}, u32[]{:S(2)}, u32[]{:S(2)}) collective-permute-start(bf16[576,256]{1,0:T(8,128)(2,1)S(1)} %collective-permute-done.19), channel_id=1, source_target_pairs={{0,7},{1,0},{2,1},{3,2},{4,3},{5,4},{6,5},{7,6},{8,15},{9,8},{10,9... | collective-permute-start | bytes 884744 | tf_op jit(solution)/shard_map/ppermute | solution.py:37
  252.2 6.3 %collective-permute-done.17 = bf16[576,256]{1,0:T(8,128)(2,1)S(1)} collective-permute-done((bf16[576,256]{1,0:T(8,128)(2,1)S(1)}, bf16[576,256]{1,0:T(8,128)(2,1)S(1)}, u32[]{:S(2)}, u32[]{:S(2)}) %collective-permute-start.17) | collective-permute-done | bytes 294944 | tf_op jit(solution)/shard_map/ppermute | solution.py:37
  258.6 3.2 %collective-permute-start.21 = (bf16[576,256]{1,0:T(8,128)(2,1)S(1)}, bf16[576,256]{1,0:T(8,128)(2,1)S(1)}, u32[]{:S(2)}, u32[]{:S(2)}) collective-permute-start(bf16[576,256]{1,0:T(8,128)(2,1)S(1)} %collective-permute-done.20), channel_id=1, source_target_pairs={{0,7},{1,0},{2,1},{3,2},{4,3},{5,4},{6,5},{7,6},{8,15},{9,8},{10,9... | collective-permute-start | bytes 884744 | tf_op jit(solution)/shard_map/ppermute | solution.py:37
  262.2 5.5 %collective-permute-done.18 = bf16[576,256]{1,0:T(8,128)(2,1)S(1)} collective-permute-done((bf16[576,256]{1,0:T(8,128)(2,1)S(1)}, bf16[576,256]{1,0:T(8,128)(2,1)S(1)}, u32[]{:S(2)}, u32[]{:S(2)}) %collective-permute-start.18) | collective-permute-done | bytes 294944 | tf_op jit(solution)/shard_map/ppermute | solution.py:37
  267.8 3.5 %collective-permute-start.23 = (bf16[288,256]{1,0:T(8,128)(2,1)S(1)}, bf16[288,256]{1,0:T(8,128)(2,1)S(1)}, u32[]{:S(2)}, u32[]{:S(2)}) collective-permute-start(bf16[288,256]{1,0:T(8,128)(2,1)S(1)} %slice.173), channel_id=1, source_target_pairs={{0,7},{1,0},{2,1},{3,2},{4,3},{5,4},{6,5},{7,6},{8,15},{9,8},{10,9... | collective-permute-start | bytes 442376 | tf_op jit(solution)/shard_map/ppermute | solution.py:37
  (194 shorter events, 67.2 us)
Async XLA Ops:
  7.2 103.5 %all-gather.5.cloned.1.call-start = ((), (), s32[]{:S(2)}) async-start(), calls=%async_computation.2 | async-start | bytes 1769472 | tf_op jit(solution)/shard_map/all_gather | solution.py:272
  17.0 19.7 %all-to-all-start = ((bf16[32,20,512]{2,1,0:T(8,128)(2,1)}), bf16[32,20,512]{2,1,0:T(8,128)(2,1)S(1)}, u32[]{:S(2)}, u32[]{:S(2)}) async-start(bf16[32,20,512]{2,1,0:T(8,128)(2,1)} %concatenate.39), calls=%async_computation | async-start | bytes 1572864 | tf_op jit(solution)/shard_map/all_to_all | solution.py:301
  24.7 252.9 %all-gather.7.cloned.1.call-start = ((), (), s32[]{:S(2)}) async-start(), calls=%async_computation.3 | async-start | bytes 2162688 | tf_op jit(solution)/shard_map/all_gather | solution.py:383
  40.8 15.7 %collective-permute-start = (bf16[288,512]{1,0:T(8,128)(2,1)S(1)}, bf16[288,512]{1,0:T(8,128)(2,1)S(1)}, u32[]{:S(2)}, u32[]{:S(2)}) collective-permute-start(bf16[288,512]{1,0:T(8,128)(2,1)S(1)} %pad_maximum_fusion.u0), channel_id=1, source_target_pairs={{0,1},{1,2},{2,3},{3,4},{4,5},{5,6},{6,7},{7,0},{8,9},{9,10},{10,1... | collective-permute-start | bytes 884744 | tf_op jit(solution)/shard_map/ppermute | solution.py:37
  42.8 13.7 %collective-permute-start.3 = (bf16[288,512]{1,0:T(8,128)(2,1)S(1)}, bf16[288,512]{1,0:T(8,128)(2,1)S(1)}, u32[]{:S(2)}, u32[]{:S(2)}) collective-permute-start(bf16[288,512]{1,0:T(8,128)(2,1)S(1)} %pad_maximum_fusion.u0), channel_id=1, source_target_pairs={{0,7},{1,0},{2,1},{3,2},{4,3},{5,4},{6,5},{7,6},{8,15},{9,8},{10,9... | collective-permute-start | bytes 884744 | tf_op jit(solution)/shard_map/ppermute | solution.py:37
  56.5 10.3 %collective-permute-start.1 = (bf16[288,512]{1,0:T(8,128)(2,1)S(1)}, bf16[288,512]{1,0:T(8,128)(2,1)}, u32[]{:S(2)}, u32[]{:S(2)}) collective-permute-start(bf16[288,512]{1,0:T(8,128)(2,1)S(1)} %collective-permute-done.u1), channel_id=1, source_target_pairs={{0,1},{1,2},{2,3},{3,4},{4,5},{5,6},{6,7},{7,0},{8,9},{9,10},{10,1... | collective-permute-start | bytes 884744 | tf_op jit(solution)/shard_map/ppermute | solution.py:37
  56.5 10.3 %collective-permute-start.4 = (bf16[288,512]{1,0:T(8,128)(2,1)S(1)}, bf16[288,512]{1,0:T(8,128)(2,1)}, u32[]{:S(2)}, u32[]{:S(2)}) collective-permute-start(bf16[288,512]{1,0:T(8,128)(2,1)S(1)} %collective-permute-done.3.d1), channel_id=1, source_target_pairs={{0,7},{1,0},{2,1},{3,2},{4,3},{5,4},{6,5},{7,6},{8,15},{9,8},{10,9... | collective-permute-start | bytes 884744 | tf_op jit(solution)/shard_map/ppermute | solution.py:37
  66.8 9.6 %collective-permute-start.2 = (bf16[288,512]{1,0:T(8,128)(2,1)}, bf16[288,512]{1,0:T(8,128)(2,1)S(1)}, u32[]{:S(2)}, u32[]{:S(2)}) collective-permute-start(bf16[288,512]{1,0:T(8,128)(2,1)} %collective-permute-done.1.u2), channel_id=1, source_target_pairs={{0,1},{1,2},{2,3},{3,4},{4,5},{5,6},{6,7},{7,0},{8,9},{9,10},{10,1... | collective-permute-start | bytes 884744 | tf_op jit(solution)/shard_map/ppermute | solution.py:37
  66.8 10.3 %collective-permute-start.5 = (bf16[288,512]{1,0:T(8,128)(2,1)}, bf16[288,512]{1,0:T(8,128)(2,1)S(1)}, u32[]{:S(2)}, u32[]{:S(2)}) collective-permute-start(bf16[288,512]{1,0:T(8,128)(2,1)} %collective-permute-done.4.d2), channel_id=1, source_target_pairs={{0,7},{1,0},{2,1},{3,2},{4,3},{5,4},{6,5},{7,6},{8,15},{9,8},{10,9... | collective-permute-start | bytes 884744 | tf_op jit(solution)/shard_map/ppermute | solution.py:37
  77.1 33.5 %collective-permute-start.6 = (bf16[144,512]{1,0:T(8,128)(2,1)}, bf16[144,512]{1,0:T(8,128)(2,1)}, u32[]{:S(2)}, u32[]{:S(2)}) collective-permute-start(bf16[144,512]{1,0:T(8,128)(2,1)} %slice.152), channel_id=1, source_target_pairs={{0,1},{1,2},{2,3},{3,4},{4,5},{5,6},{6,7},{7,0},{8,9},{9,10},{10,1... | collective-permute-start | bytes 442376 | tf_op jit(solution)/shard_map/ppermute | solution.py:37
  77.8 32.9 %collective-permute-start.7 = (bf16[144,512]{1,0:T(8,128)(2,1)}, bf16[144,512]{1,0:T(8,128)(2,1)}, u32[]{:S(2)}, u32[]{:S(2)}) collective-permute-start(bf16[144,512]{1,0:T(8,128)(2,1)} %slice.153), channel_id=1, source_target_pairs={{0,7},{1,0},{2,1},{3,2},{4,3},{5,4},{6,5},{7,6},{8,15},{9,8},{10,9... | collective-permute-start | bytes 442376 | tf_op jit(solution)/shard_map/ppermute | solution.py:37
  129.4 14.3 %collective-permute-start.12 = (bf16[2,2,512,128]{3,2,0,1:T(8,128)(2,1)}, bf16[2,2,512,128]{3,2,0,1:T(8,128)(2,1)}, u32[]{:S(2)}, u32[]{:S(2)}) collective-permute-start(bf16[2,2,512,128]{3,2,0,1:T(8,128)(2,1)} %fusion.8), channel_id=1, source_target_pairs={{0,64},{64,128},{128,192},{192,0},{1,65},{65,129},{129,193},{193,1... | collective-permute-start | bytes 1572872 | tf_op jit(solution)/shard_map/ppermute | solution.py:37
  130.9 14.9 %collective-permute-start.13 = (bf16[2,2,512,128]{3,2,0,1:T(8,128)(2,1)}, bf16[2,2,512,128]{3,2,0,1:T(8,128)(2,1)}, u32[]{:S(2)}, u32[]{:S(2)}) collective-permute-start(bf16[2,2,512,128]{3,2,0,1:T(8,128)(2,1)} %fusion.8), channel_id=1, source_target_pairs={{0,192},{64,0},{128,64},{192,128},{1,193},{65,1},{129,65},{193,129... | collective-permute-start | bytes 1572872 | tf_op jit(solution)/shard_map/ppermute | solution.py:37
  135.5 19.4 %collective-permute-start.10 = (bf16[2,512,128]{2,1,0:T(8,128)(2,1)S(1)}, bf16[2,512,128]{2,1,0:T(8,128)(2,1)S(1)}, u32[]{:S(2)}, u32[]{:S(2)}) collective-permute-start(bf16[2,512,128]{2,1,0:T(8,128)(2,1)S(1)} %get-tuple-element.35.q0), channel_id=1, source_target_pairs={{0,32},{16,48},{32,0},{48,16},{1,33},{17,49},{33,1},{49,17},{2,34}... | collective-permute-start | bytes 786440 | tf_op jit(solution)/shard_map/ppermute | solution.py:37
  136.1 18.7 %collective-permute-start.11 = (bf16[2,512,128]{2,1,0:T(8,128)(2,1)S(1)}, bf16[2,512,128]{2,1,0:T(8,128)(2,1)S(1)}, u32[]{:S(2)}, u32[]{:S(2)}) collective-permute-start(bf16[2,512,128]{2,1,0:T(8,128)(2,1)S(1)} %get-tuple-element.35.q0), channel_id=1, source_target_pairs={{0,48},{16,0},{32,16},{48,32},{1,49},{17,1},{33,17},{49,33},{2,50}... | collective-permute-start | bytes 786440 | tf_op jit(solution)/shard_map/ppermute | solution.py:37
  139.3 19.3 %collective-permute-start.9 = (bf16[2,512,128]{2,1,0:T(8,128)(2,1)S(1)}, bf16[2,512,128]{2,1,0:T(8,128)(2,1)S(1)}, u32[]{:S(2)}, u32[]{:S(2)}) collective-permute-start(bf16[2,512,128]{2,1,0:T(8,128)(2,1)S(1)} %get-tuple-element.35.q0), channel_id=1, source_target_pairs={{0,16},{16,32},{32,48},{48,0},{1,17},{17,33},{33,49},{49,1},{2,18}... | collective-permute-start | bytes 786440 | tf_op jit(solution)/shard_map/ppermute | solution.py:37
  143.7 11.2 %collective-permute-start.14 = (bf16[2,512,128]{2,1,0:T(8,128)(2,1)}, bf16[2,512,128]{2,1,0:T(8,128)(2,1)S(1)}, u32[]{:S(2)}, u32[]{:S(2)}) collective-permute-start(bf16[2,512,128]{2,1,0:T(8,128)(2,1)} %get-tuple-element.36), channel_id=1, source_target_pairs={{0,128},{64,192},{128,0},{192,64},{1,129},{65,193},{129,1},{193,65... | collective-permute-start | bytes 786440 | tf_op jit(solution)/shard_map/ppermute | solution.py:37
  145.8 12.9 %collective-permute-start.15 = (bf16[2,512,128]{2,1,0:T(8,128)(2,1)}, bf16[2,512,128]{2,1,0:T(8,128)(2,1)}, u32[]{:S(2)}, u32[]{:S(2)}) collective-permute-start(bf16[2,512,128]{2,1,0:T(8,128)(2,1)} %get-tuple-element.34), channel_id=1, source_target_pairs={{0,128},{64,192},{128,0},{192,64},{1,129},{65,193},{129,1},{193,65... | collective-permute-start | bytes 786440 | tf_op jit(solution)/shard_map/ppermute | solution.py:37
  213.6 23.3 %all-to-all-start.1 = ((bf16[32,10,16,128]{3,2,1,0:T(8,128)(2,1)}), bf16[32,10,16,128]{3,2,1,0:T(8,128)(2,1)S(1)}, u32[]{:S(2)}, u32[]{:S(2)}) async-start(bf16[32,10,16,128]{3,2,1,0:T(8,128)(2,1)} %copy-done.1), calls=%async_computation.1 | async-start | bytes 2621440 | tf_op jit(solution)/shard_map/all_to_all | solution.py:380
  237.7 10.9 %collective-permute-start.16 = (bf16[576,256]{1,0:T(8,128)(2,1)S(1)}, bf16[576,256]{1,0:T(8,128)(2,1)S(1)}, u32[]{:S(2)}, u32[]{:S(2)}) collective-permute-start(bf16[576,256]{1,0:T(8,128)(2,1)S(1)} %get-tuple-element.13), channel_id=1, source_target_pairs={{0,1},{1,2},{2,3},{3,4},{4,5},{5,6},{6,7},{7,0},{8,9},{9,10},{10,1... | collective-permute-start | bytes 884744 | tf_op jit(solution)/shard_map/ppermute | solution.py:37
  237.8 10.8 %collective-permute-start.19 = (bf16[576,256]{1,0:T(8,128)(2,1)S(1)}, bf16[576,256]{1,0:T(8,128)(2,1)S(1)}, u32[]{:S(2)}, u32[]{:S(2)}) collective-permute-start(bf16[576,256]{1,0:T(8,128)(2,1)S(1)} %get-tuple-element.13), channel_id=1, source_target_pairs={{0,7},{1,0},{2,1},{3,2},{4,3},{5,4},{6,5},{7,6},{8,15},{9,8},{10,9... | collective-permute-start | bytes 884744 | tf_op jit(solution)/shard_map/ppermute | solution.py:37
  248.6 10.0 %collective-permute-start.17 = (bf16[576,256]{1,0:T(8,128)(2,1)S(1)}, bf16[576,256]{1,0:T(8,128)(2,1)S(1)}, u32[]{:S(2)}, u32[]{:S(2)}) collective-permute-start(bf16[576,256]{1,0:T(8,128)(2,1)S(1)} %collective-permute-done.16), channel_id=1, source_target_pairs={{0,1},{1,2},{2,3},{3,4},{4,5},{5,6},{6,7},{7,0},{8,9},{9,10},{10,1... | collective-permute-start | bytes 884744 | tf_op jit(solution)/shard_map/ppermute | solution.py:37
  248.6 10.0 %collective-permute-start.20 = (bf16[576,256]{1,0:T(8,128)(2,1)S(1)}, bf16[576,256]{1,0:T(8,128)(2,1)S(1)}, u32[]{:S(2)}, u32[]{:S(2)}) collective-permute-start(bf16[576,256]{1,0:T(8,128)(2,1)S(1)} %collective-permute-done.19), channel_id=1, source_target_pairs={{0,7},{1,0},{2,1},{3,2},{4,3},{5,4},{6,5},{7,6},{8,15},{9,8},{10,9... | collective-permute-start | bytes 884744 | tf_op jit(solution)/shard_map/ppermute | solution.py:37
  258.6 9.2 %collective-permute-start.21 = (bf16[576,256]{1,0:T(8,128)(2,1)S(1)}, bf16[576,256]{1,0:T(8,128)(2,1)S(1)}, u32[]{:S(2)}, u32[]{:S(2)}) collective-permute-start(bf16[576,256]{1,0:T(8,128)(2,1)S(1)} %collective-permute-done.20), channel_id=1, source_target_pairs={{0,7},{1,0},{2,1},{3,2},{4,3},{5,4},{6,5},{7,6},{8,15},{9,8},{10,9... | collective-permute-start | bytes 884744 | tf_op jit(solution)/shard_map/ppermute | solution.py:37
  (40 other events, 350.8 us)
Sparse Core Ops, SparseCore 0:
  10.5 44.0 all-gather.4
  149.4 45.8 all-gather.6
